TPU v7x, 32 devices: a whole 2x2x4 slice. The times are simulated.
32 devices in a mesh: groups: 2 (over x), wide: 8 (over z, y), narrow: 2 (over core).
Axes of the slice: x: 2, y: 2, z: 4, core: 2. Of those that a mesh axis runs over, the one named last changes fastest.
Arguments:
- volume: bfloat16 [32, 128, 16, 32], P(None, ('groups', 'wide'), None, 'narrow'), parts along dimension 1, may hold values from -6 to 6
- cotangent: bfloat16 [32, 128, 16, 32], P(None, ('groups', 'wide'), None, 'narrow'), parts along dimension 1, may hold values from -6 to 6
- fine_weight: bfloat16 [27, 32, 32], replicated, may hold values from -0.21875 to 0.21875
- merge_weight: bfloat16 [16384, 1024], P('wide'), may hold values from -0.046875 to 0.046875
- hidden_weight: bfloat16 [27, 1024, 2048], P(None, None, 'wide'), may hold values from -0.0390625 to 0.0390625
- step_table: float32 [1000, 2048], P(None, 'wide'), may hold values from -6 to 6
- output_weight: bfloat16 [27, 2048, 1024], P(None, 'wide'), may hold values from -0.02734375 to 0.02734375
- expand_weight: bfloat16 [1024, 16384], P(None, 'wide'), may hold values from -0.1875 to 0.1875
- timestep: int32 [2], P('groups'), parts along dimension 0, may hold values from 0 to 999
Outputs:
- input_grad: bfloat16 [32, 128, 16, 32], P(None, ('groups', 'wide'), None, 'narrow'), parts along dimension 1
There are 2 independent parts, one for each index of `groups`. A program takes and returns all parts, laid end to end along the dimension named above; an argument that names none is the same for every part. Nothing has to cross between parts.
All inputs are finite; a program needn't handle non-finite values.
Results may differ from a plain program's by a relative error of at most 0.012.
Values may be sent and summed in bfloat16 or wider, within the bound.
No kernel may reach another device: no remote copies, remote signals or barrier semaphores. Data moves between devices by JAX's collectives and lax.ppermute only.
A program may use at most 128 MiB of HBM per device.

v0:
```python
import jax
import jax.numpy as jnp
from jax import lax
from jax.sharding import PartitionSpec as P

PATCH = 8


def extended(cells, sides, width):
    for axis, dim in sides:
        count = lax.axis_size(axis)
        ends = count - 1
        head = lax.slice_in_dim(cells, 0, width, axis=dim)
        tail = lax.slice_in_dim(cells, cells.shape[dim] - width, cells.shape[dim], axis=dim)
        cells = jnp.concatenate(
            [
                lax.ppermute(tail, axis, [(i, (i + 1) % count) for i in range(ends)]),
                cells,
                lax.ppermute(head, axis, [((i + 1) % count, i) for i in range(ends)]),
            ],
            axis=dim,
        )
    return cells


def shifts(transposed):
    return [
        (2 - i, 2 - j, 2 - k) if transposed else (i, j, k)
        for i in range(3)
        for j in range(3)
        for k in range(3)
    ]


def silu_slope(values):
    logistic = jax.nn.sigmoid(values)
    return logistic * (1.0 + values * (1.0 - logistic))


def fine_conv(fine_field, weight, transposed):
    grown = extended(fine_field, (("wide", 1), ("narrow", 3)), 1)
    padded = jnp.pad(grown, ((0, 0), (0, 0), (1, 1), (0, 0)))
    kernel = weight.reshape(3, 3, 3, weight.shape[1], weight.shape[2])
    if transposed:
        kernel = kernel[::-1, ::-1, ::-1]
    result = lax.conv_general_dilated(
        padded[None],
        kernel,
        (1, 1, 1),
        "VALID",
        dimension_numbers=("NCDHW", "DHWIO", "NCDHW"),
        preferred_element_type=jnp.float32,
    )
    return result[0]


def to_patches(fine_field):
    channels = fine_field.shape[0]
    shaped = fine_field.reshape(
        channels, PATCH, fine_field.shape[2] // PATCH, PATCH, fine_field.shape[3] // PATCH, PATCH
    )
    return shaped.transpose(2, 4, 1, 3, 5, 0).reshape(-1, PATCH**3 * channels)


def send_patches(fine_field):
    return lax.all_to_all(to_patches(fine_field), "wide", split_axis=1, concat_axis=0, tiled=True)


def return_patches(patch_rows, fine_height, fine_depth, channels):
    returned = lax.all_to_all(patch_rows, "wide", split_axis=0, concat_axis=1, tiled=True)
    shaped = returned.reshape(
        fine_height // PATCH, fine_depth // PATCH, PATCH, PATCH, PATCH, channels
    )
    return shaped.transpose(5, 2, 0, 3, 1, 4).reshape(channels, PATCH, fine_height, fine_depth)


def coarse_faces(coarse_block):
    return extended(coarse_block, (("narrow", 2),), 1)


def wide_input_conv(coarse_block, weight_mat, out_count, transposed):
    grown = coarse_faces(coarse_block)
    products = jnp.einsum("xyzd,dk->xyzk", grown, weight_mat, preferred_element_type=jnp.float32)
    padded = jnp.pad(products, ((1, 1), (1, 1), (0, 0), (0, 0)))
    extent = coarse_block.shape[:3]
    summed = jnp.zeros(extent + (out_count,), jnp.float32)
    for tap_index, (a, b, c) in enumerate(shifts(transposed)):
        summed = (
            summed
            + padded[
                a : a + extent[0],
                b : b + extent[1],
                c : c + extent[2],
                tap_index * out_count : (tap_index + 1) * out_count,
            ]
        )
    return summed


def narrow_input_conv(coarse_block, weight_mat, transposed):
    grown = coarse_faces(coarse_block)
    padded = jnp.pad(grown, ((1, 1), (1, 1), (0, 0), (0, 0)))
    extent = coarse_block.shape[:3]
    columns = jnp.concatenate(
        [
            padded[a : a + extent[0], b : b + extent[1], c : c + extent[2]]
            for a, b, c in shifts(transposed)
        ],
        axis=3,
    )
    return jnp.einsum("xyzk,kd->xyzd", columns, weight_mat, preferred_element_type=jnp.float32)


def shards(
    volume,
    cotangent,
    fine_weight,
    merge_weight,
    hidden_weight,
    step_table,
    output_weight,
    expand_weight,
    timestep,
):
    channels = volume.shape[0]
    fine_height = volume.shape[2]
    fine_depth = volume.shape[3]
    wide_count = lax.axis_size("wide")
    features = merge_weight.shape[1]
    hidden_local = hidden_weight.shape[2]
    coarse_grid = (wide_count, fine_height // PATCH, fine_depth // PATCH)
    hidden_mat = hidden_weight.transpose(1, 0, 2).reshape(features, 27 * hidden_local)
    output_mat = output_weight.reshape(27 * hidden_local, features)
    output_back = output_weight.transpose(2, 0, 1).reshape(features, 27 * hidden_local)
    hidden_back = hidden_weight.transpose(0, 2, 1).reshape(27 * hidden_local, features)

    def total_rows(partial_value):
        return lax.psum(partial_value, "wide")

    pre_act = fine_conv(volume, fine_weight, False)
    activated = jax.nn.silu(pre_act).astype(jnp.bfloat16)
    received = send_patches(activated)
    merged = total_rows(jnp.dot(received, merge_weight, preferred_element_type=jnp.float32))
    coarse_in = merged.astype(jnp.bfloat16).reshape(coarse_grid + (features,))
    bias_row = step_table[timestep[0]]
    gate_pre = wide_input_conv(coarse_in, hidden_mat, hidden_local, False) + bias_row
    hidden_act = jax.nn.silu(gate_pre).astype(jnp.bfloat16)
    branch = total_rows(narrow_input_conv(hidden_act, output_mat, False).reshape(-1, features))
    residual_sum = (merged + branch).astype(jnp.bfloat16)
    expanded = jnp.dot(residual_sum, expand_weight, preferred_element_type=jnp.float32).astype(
        jnp.bfloat16
    )
    expanded_field = return_patches(expanded, fine_height, fine_depth, channels)
    combined = activated.astype(jnp.float32) + expanded_field.astype(jnp.float32)
    grad_comb = (cotangent.astype(jnp.float32) * silu_slope(combined)).astype(jnp.bfloat16)
    grad_res = total_rows(
        jnp.einsum(
            "nk,dk->nd", send_patches(grad_comb), expand_weight, preferred_element_type=jnp.float32
        )
    )
    grad_res_b = grad_res.astype(jnp.bfloat16).reshape(coarse_grid + (features,))
    grad_hidden = wide_input_conv(grad_res_b, output_back, hidden_local, True)
    grad_gate = (grad_hidden * silu_slope(gate_pre)).astype(jnp.bfloat16)
    grad_conv = total_rows(narrow_input_conv(grad_gate, hidden_back, True).reshape(-1, features))
    grad_merged = (grad_res + grad_conv).astype(jnp.bfloat16)
    grad_cells = jnp.einsum(
        "nd,kd->nk", grad_merged, merge_weight, preferred_element_type=jnp.float32
    ).astype(jnp.bfloat16)
    grad_act = return_patches(grad_cells, fine_height, fine_depth, channels).astype(
        jnp.float32
    ) + grad_comb.astype(jnp.float32)
    grad_pre = (grad_act * silu_slope(pre_act)).astype(jnp.bfloat16)
    return fine_conv(grad_pre, fine_weight.transpose(0, 2, 1), True).astype(jnp.bfloat16)


def solution(mesh):
    in_specs = (
        P(None, ("groups", "wide"), None, "narrow"),
        P(None, ("groups", "wide"), None, "narrow"),
        P(),
        P("wide", None),
        P(None, None, "wide"),
        P(None, "wide"),
        P(None, "wide", None),
        P(None, "wide"),
        P("groups"),
    )
    out_specs = P(None, ("groups", "wide"), None, "narrow")
    return jax.shard_map(shards, mesh=mesh, in_specs=in_specs, out_specs=out_specs, check_vma=False)
```

profile of v0, /device:TPU:0, one launch (start us, length us, event | category | flops | bytes accessed | tf_op | source)
XLA Modules:
  0.0 473.5 jit_solution(18221159646353453401)
XLA Ops:
  7.5 4.9 %collective-permute-start = (bf16[32,1,16,16]{0,3,2,1:T(8,128)(2,1)S(1)}, bf16[32,1,16,16]{0,3,2,1:T(8,128)(2,1)S(1)}, u32[]{:S(2)}, u32[]{:S(2)}) collective-permute-start(bf16[32,1,16,16]{0,3,2,1:T(8,128)(2,1)S(1)} %get-tuple-element.14), channel_id=1, source_target_pairs={{0,2},{2,4},{4,6},{6,8},{8,10},{10,12},{12,14},{1,3},{3,5},{5,7},{... | collective-permute-start | bytes 49160 | tf_op jit(solution)/shard_map/ppermute | solution.py:17
  12.4 1.3 collective-permute-start.1
  15.4 3.2 collective-permute-done.1
  18.7 1.3 collective-permute-start.2
  20.0 1.3 collective-permute-start.3
  21.3 1.9 collective-permute-done.3
  23.7 1.3 pad.27
  25.0 2.8 reshape.76
  28.8 2.4 fusion.20
  32.6 12.9 %all_to_all.64 = bf16[4,8,2048]{2,0,1:T(4,128)(2,1)S(1)} all-to-all(bf16[4,8,2048]{2,0,1:T(4,128)(2,1)S(1)} %copy.53), channel_id=1, replica_groups=mesh['groups'=2,'wide'=8,'narrow'=2] {'wide'}, dimensions={1} | all-to-all | bytes 262144 | tf_op jit(solution)/shard_map/all_to_all | solution.py:66
  45.5 3.7 fusion.129
  50.0 67.2 %all-reduce.11.cloned.1.call-done = f32[32,1024]{1,0:T(8,128)} async-done(((f32[32,1024]{1,0:T(8,128)}), f32[32,1024]{1,0:T(8,128)}) %all-reduce.11.cloned.1.call-update) | async-done | bytes 131088 | tf_op jit(solution)/shard_map/psum | solution.py:138
  118.1 1.3 collective-permute-start.4
  119.4 1.3 collective-permute-start.5
  120.7 18.6 %copy.57 = bf16[27,1024,256]{1,2,0:T(8,128)(2,1)} copy(bf16[27,1024,256]{2,1,0:T(8,128)(2,1)} %param.13) | data formatting | bytes 28311552 | tf_op args[4]
  139.4 9.4 %fusion.50 = f32[8,2,4,6912]{3,0,2,1:T(8,128)S(1)} fusion(bf16[1024,6912,1,1]{0,1,3,2:T(8,128)(2,1)} %bitcast.118, bf16[8,2,1,1024]{3,0,2,1:T(8,128)(2,1)S(1)} %collective-permute-done.5, bf16[8,2,2,1024]{3,0,2,1:T(8,128)(2,1)S(1)} %copy.54, bf16[8,2,1,1024]{3,0,2,1:T(8,128)(2,1)S(1)} %collective-permute-done.4), kind=kOutput, calls=%fused_computation.119 | convolution fusion | flops 906100736 | bytes 16056320 | tf_op jit(solution)/shard_map/xyzd,dk->xyzk/dot_general | solution.py:83
  148.9 3.0 collective-permute-start.6
  151.9 1.5 collective-permute-start.7
  153.4 1.6 collective-permute-done.7
  155.9 8.3 %fusion.130 = f32[32,1024]{1,0:T(8,128)} fusion(bf16[32,6912]{1,0:T(8,128)(2,1)S(1)} %dot_general.30, bf16[6912,1024]{1,0:T(8,128)(2,1)} %bitcast.120), kind=kOutput, calls=%fused_computation.271 | convolution fusion | flops 452984832 | bytes 14729216 | tf_op jit(solution)/shard_map/xyzk,kd->xyzd/dot_general | solution.py:111
  164.3 69.0 %all-reduce.13.cloned.1.call-done = f32[32,1024]{1,0:T(8,128)} async-done(((f32[32,1024]{1,0:T(8,128)}), f32[32,1024]{1,0:T(8,128)}) %all-reduce.13.cloned.1.call-update) | async-done | bytes 131088 | tf_op jit(solution)/shard_map/psum | solution.py:138
  233.3 3.1 convolution_convert_fusion.1
  236.4 11.1 %all_to_all.65 = bf16[8,4,2048]{2,1,0:T(4,128)(2,1)S(1)} all-to-all(bf16[8,4,2048]{2,1,0:T(4,128)(2,1)S(1)} %all_to_all.52), channel_id=1, replica_groups=mesh['groups'=2,'wide'=8,'narrow'=2] {'wide'}, dimensions={0} | all-to-all | bytes 262144 | tf_op jit(solution)/shard_map/all_to_all | solution.py:70
  247.6 1.4 reshape.100
  249.0 1.4 copy.60
  251.9 9.7 %all_to_all.66 = bf16[4,8,2048]{2,0,1:T(4,128)(2,1)S(1)} all-to-all(bf16[4,8,2048]{2,0,1:T(4,128)(2,1)S(1)} %copy.62), channel_id=1, replica_groups=mesh['groups'=2,'wide'=8,'narrow'=2] {'wide'}, dimensions={1} | all-to-all | bytes 262144 | tf_op jit(solution)/shard_map/all_to_all | solution.py:66
  261.6 4.2 fusion.131
  265.9 67.4 %all-reduce.15.cloned.1.call-done = f32[32,1024]{1,0:T(8,128)} async-done(((f32[32,1024]{1,0:T(8,128)}), f32[32,1024]{1,0:T(8,128)}) %all-reduce.15.cloned.1.call-update) | async-done | bytes 131088 | tf_op jit(solution)/shard_map/psum | solution.py:138
  334.3 1.3 collective-permute-start.8
  335.6 1.3 collective-permute-start.9
  336.9 1.8 collective-permute-done.9
  338.7 9.4 %fusion.56 = f32[8,2,4,6912]{3,0,2,1:T(8,128)S(1)} fusion(bf16[1024,6912,1,1]{0,1,3,2:T(8,128)(2,1)} %bitcast.121, bf16[8,2,1,1024]{3,0,2,1:T(8,128)(2,1)S(1)} %collective-permute-done.9, bf16[8,2,2,1024]{3,0,2,1:T(8,128)(2,1)S(1)} %copy.63, bf16[8,2,1,1024]{3,0,2,1:T(8,128)(2,1)S(1)} %collective-permute-done.8), kind=kOutput, calls=%fused_computation.125 | convolution fusion | flops 906100736 | bytes 16056320 | tf_op jit(solution)/shard_map/xyzd,dk->xyzk/dot_general | solution.py:83
  348.2 2.1 collective-permute-start.10
  350.3 1.5 collective-permute-start.11
  351.8 1.5 collective-permute-done.11
  354.3 8.2 %fusion.132 = f32[32,1024]{1,0:T(8,128)} fusion(bf16[32,6912]{1,0:T(8,128)(2,1)S(1)} %dot_general.35, bf16[6912,1024]{1,0:T(8,128)(2,1)} %bitcast.119), kind=kOutput, calls=%fused_computation.273 | convolution fusion | flops 452984832 | bytes 14729216 | tf_op jit(solution)/shard_map/xyzk,kd->xyzd/dot_general | solution.py:111
  362.6 69.0 %all-reduce.17.cloned.1.call-done = f32[32,1024]{1,0:T(8,128)} async-done(((f32[32,1024]{1,0:T(8,128)}), f32[32,1024]{1,0:T(8,128)}) %all-reduce.17.cloned.1.call-update) | async-done | bytes 131088 | tf_op jit(solution)/shard_map/psum | solution.py:138
  431.6 3.6 convolution_convert_fusion
  435.3 11.0 %all_to_all.67 = bf16[8,4,2048]{2,1,0:T(4,128)(2,1)S(1)} all-to-all(bf16[8,4,2048]{2,1,0:T(4,128)(2,1)S(1)} %all_to_all.58), channel_id=1, replica_groups=mesh['groups'=2,'wide'=8,'narrow'=2] {'wide'}, dimensions={0} | all-to-all | bytes 262144 | tf_op jit(solution)/shard_map/all_to_all | solution.py:70
  446.3 1.3 reshape.101
  447.7 1.4 copy.69
  449.5 2.1 collective-permute-start.12
  451.7 1.3 collective-permute-start.13
  453.6 4.3 collective-permute-done.13
  457.9 1.3 collective-permute-start.14
  459.2 1.3 collective-permute-start.15
  460.5 1.8 collective-permute-done.15
  463.5 2.3 select_convert_fusion
  (137 shorter events, 14.6 us)
Async XLA Ops:
  6.5 114.2 %copy-start = (f32[1000,256]{1,0:T(8,128)S(1)}, f32[1000,256]{1,0:T(8,128)}, u32[]{:S(2)}) copy-start(f32[1000,256]{1,0:T(8,128)} %param.14) | copy-start | bytes 3072004
  6.5 110.6 %all-reduce.11.cloned.1.call-start = ((), (), s32[]{:S(2)}) async-start(), calls=%async_computation.4 | async-start | bytes 262144 | tf_op jit(solution)/shard_map/psum | solution.py:138
  7.5 6.8 %collective-permute-start = (bf16[32,1,16,16]{0,3,2,1:T(8,128)(2,1)S(1)}, bf16[32,1,16,16]{0,3,2,1:T(8,128)(2,1)S(1)}, u32[]{:S(2)}, u32[]{:S(2)}) collective-permute-start(bf16[32,1,16,16]{0,3,2,1:T(8,128)(2,1)S(1)} %get-tuple-element.14), channel_id=1, source_target_pairs={{0,2},{2,4},{4,6},{6,8},{8,10},{10,12},{12,14},{1,3},{3,5},{5,7},{... | collective-permute-start | bytes 49160 | tf_op jit(solution)/shard_map/ppermute | solution.py:17
  12.4 6.2 %collective-permute-start.1 = (bf16[32,1,16,16]{0,3,2,1:T(8,128)(2,1)S(1)}, bf16[32,1,16,16]{0,3,2,1:T(8,128)(2,1)S(1)}, u32[]{:S(2)}, u32[]{:S(2)}) collective-permute-start(bf16[32,1,16,16]{0,3,2,1:T(8,128)(2,1)S(1)} %get-tuple-element.13), channel_id=1, source_target_pairs={{2,0},{4,2},{6,4},{8,6},{10,8},{12,10},{14,12},{3,1},{5,3},{7,5},{... | collective-permute-start | bytes 49160 | tf_op jit(solution)/shard_map/ppermute | solution.py:19
  18.7 2.6 collective-permute-start.2
  20.0 3.2 collective-permute-start.3
  27.8 0.9 copy-start.5
  27.9 0.9 copy-start.6
  49.3 184.0 %all-reduce.13.cloned.1.call-start = ((), (), s32[]{:S(2)}) async-start(), calls=%async_computation.5 | async-start | bytes 262144 | tf_op jit(solution)/shard_map/psum | solution.py:138
  118.1 21.3 %collective-permute-start.4 = (bf16[8,2,1,1024]{3,0,2,1:T(8,128)(2,1)S(1)}, bf16[8,2,1,1024]{3,0,2,1:T(8,128)(2,1)S(1)}, u32[]{:S(2)}, u32[]{:S(2)}) collective-permute-start(bf16[8,2,1,1024]{3,0,2,1:T(8,128)(2,1)S(1)} %get-tuple-element.17), channel_id=1, source_target_pairs={{0,1},{2,3},{4,5},{6,7},{8,9},{10,11},{12,13},{14,15},{16,17},{18,... | collective-permute-start | bytes 98312 | tf_op jit(solution)/shard_map/ppermute | solution.py:17
  119.4 20.0 %collective-permute-start.5 = (bf16[8,2,1,1024]{3,0,2,1:T(8,128)(2,1)S(1)}, bf16[8,2,1,1024]{3,0,2,1:T(8,128)(2,1)S(1)}, u32[]{:S(2)}, u32[]{:S(2)}) collective-permute-start(bf16[8,2,1,1024]{3,0,2,1:T(8,128)(2,1)S(1)} %get-tuple-element.18), channel_id=1, source_target_pairs={{1,0},{3,2},{5,4},{7,6},{9,8},{11,10},{13,12},{15,14},{17,16},{19,... | collective-permute-start | bytes 98312 | tf_op jit(solution)/shard_map/ppermute | solution.py:19
  148.9 4.5 collective-permute-start.6
  151.9 3.1 collective-permute-start.7
  155.9 77.3 %copy-start.2 = (f32[32,1024]{1,0:T(8,128)S(1)}, f32[32,1024]{1,0:T(8,128)}, u32[]{:S(2)}) copy-start(f32[32,1024]{1,0:T(8,128)} %all-reduce.11.cloned.1.call-done) | copy-start | bytes 393220
  164.2 169.1 %all-reduce.15.cloned.1.call-start = ((), (), s32[]{:S(2)}) async-start(), calls=%async_computation.6 | async-start | bytes 262144 | tf_op jit(solution)/shard_map/psum | solution.py:138
  236.4 14.0 %copy-start.4 = (bf16[32,8,16,16]{0,3,2,1:T(8,128)(2,1)S(1)}, bf16[32,8,16,16]{0,3,2,1:T(8,128)(2,1)}, u32[]{:S(2)}) copy-start(bf16[32,8,16,16]{0,3,2,1:T(8,128)(2,1)} %param.10) | copy-start | bytes 393220
  265.8 165.8 %all-reduce.17.cloned.1.call-start = ((), (), s32[]{:S(2)}) async-start(), calls=%async_computation.7 | async-start | bytes 262144 | tf_op jit(solution)/shard_map/psum | solution.py:138
  334.3 2.6 collective-permute-start.8
  335.6 3.1 collective-permute-start.9
  348.2 3.6 collective-permute-start.10
  350.3 3.1 collective-permute-start.11
  354.3 77.3 %copy-start.3 = (f32[32,1024]{1,0:T(8,128)S(1)}, f32[32,1024]{1,0:T(8,128)}, u32[]{:S(2)}) copy-start(f32[32,1024]{1,0:T(8,128)} %all-reduce.15.cloned.1.call-done) | copy-start | bytes 393220
  449.5 4.0 collective-permute-start.12
  451.7 6.2 %collective-permute-start.13 = (bf16[32,1,16,16]{0,2,3,1:T(8,128)(2,1)S(1)}, bf16[32,1,16,16]{0,2,3,1:T(8,128)(2,1)S(1)}, u32[]{:S(2)}, u32[]{:S(2)}) collective-permute-start(bf16[32,1,16,16]{0,2,3,1:T(8,128)(2,1)S(1)} %get-tuple-element.12), channel_id=1, source_target_pairs={{2,0},{4,2},{6,4},{8,6},{10,8},{12,10},{14,12},{3,1},{5,3},{7,5},{... | collective-permute-start | bytes 49160 | tf_op jit(solution)/shard_map/ppermute | solution.py:19
  457.9 2.6 collective-permute-start.14
  459.2 3.1 collective-permute-start.15
  463.5 3.4 copy-start.1
Sparse Core Ops, SparseCore 0:
  49.4 67.6 all-reduce.10
  164.3 68.8 all-reduce.12
  266.0 67.3 all-reduce.14
  362.7 68.8 all-reduce.16
where the time goes:
time: 475 us; the launch traced here: 473 us
  waiting for transfers between devices  290 us (61%)
  matrix products  54.5 us (11%)
  blocking collectives  44.8 us (9%)
  local copies, waits for them, and re-layouts  36.7 us (8%)
  starting transfers between devices  28.1 us (6%)
  between operations  14.8 us (3%)
  other arithmetic  4.77 us (1%)
    psum x4, waiting for transfers between devices, total_rows(): return lax.psum(partial_value, 'wide')  273 us
    all_to_all x2, blocking collectives, send_patches(): lax.all_to_all(to_patches(fine_field), 'wide', split_axis=1, concat_axis=...  22.6 us
    all_to_all x2, blocking collectives, return_patches(): lax.all_to_all(patch_rows, 'wide', split_axis=0, concat_axis=1, tiled=True)  22.2 us
    unnamed x65, local copies, waits for them, and re-layouts  20.7 us
    dot_general x2, matrix products, wide_input_conv(): jnp.einsum('xyzd,dk->xyzk', grown, weight_mat, preferred_element_type=jnp...  18.8 us
    ppermute x8, starting transfers between devices, extended(): lax.ppermute(tail, axis, [(i, (i + 1) % count) for i in range(ends)])  17.3 us
    dot_general x2, matrix products, narrow_input_conv(): jnp.einsum('xyzk,kd->xyzd', columns, weight_mat, preferred_element_type=j...  16.5 us
    ppermute x8, waiting for transfers between devices, extended(): lax.ppermute(head, axis, [((i + 1) % count, i) for i in range(ends)])  16 us
  transfers between devices with their start and end apart: 20, of which 13 were waited for; matrix products, arithmetic and copies ran while one was open for 4% of the time, Pallas kernels for 0%

commit v1 on v0

--- a/solution.py
+++ b/solution.py
@@ -135,7 +135,7 @@
     hidden_back = hidden_weight.transpose(0, 2, 1).reshape(27 * hidden_local, features)
 
     def total_rows(partial_value):
-        return lax.psum(partial_value, "wide")
+        return jnp.sum(lax.all_gather(partial_value, "wide"), axis=0)
 
     pre_act = fine_conv(volume, fine_weight, False)
     activated = jax.nn.silu(pre_act).astype(jnp.bfloat16)

time: 475 us -> 358 us (0.75)
  waiting for transfers between devices: 290 us -> 171 us
    psum x4 -> x0, waiting for transfers between devices: 273 us -> none  [total_rows(): return lax.psum(partial_value, 'wide')]
    all_gather x0 -> x4, waiting for transfers between devices: none -> 154 us  [total_rows(): return jnp.sum(lax.all_gather(partial_value, 'wide'), axis=0)]
    reduce_sum x0 -> x4, other arithmetic: none -> 5.17 us  [total_rows(): return jnp.sum(lax.all_gather(partial_value, 'wide'), axis=0)]
    unnamed x65 -> x61, local copies, waits for them, and re-layouts: 20.7 us -> 20.7 us
  transfers between devices with their start and end apart: 20 -> 20, of which waited for: 13 -> 13; matrix products, arithmetic and copies ran while one was open for 4% -> 6% of each run, Pallas kernels for 0% -> 0%
where the time goes in v1:
time: 358 us; the launch traced here: 357 us
  waiting for transfers between devices  171 us (48%)
  matrix products  54.3 us (15%)
  blocking collectives  43.7 us (12%)
  local copies, waits for them, and re-layouts  36.7 us (10%)
  starting transfers between devices  28.1 us (8%)
  between operations  14.8 us (4%)
  other arithmetic  8.13 us (2%)
    all_gather x4, waiting for transfers between devices, total_rows(): return jnp.sum(lax.all_gather(partial_value, 'wide'), axis=0)  154 us
    all_to_all x2, blocking collectives, send_patches(): lax.all_to_all(to_patches(fine_field), 'wide', split_axis=1, concat_axis=...  22.6 us
    all_to_all x2, blocking collectives, return_patches(): lax.all_to_all(patch_rows, 'wide', split_axis=0, concat_axis=1, tiled=True)  21.1 us
    unnamed x61, local copies, waits for them, and re-layouts  20.7 us
    dot_general x2, matrix products, wide_input_conv(): jnp.einsum('xyzd,dk->xyzk', grown, weight_mat, preferred_element_type=jnp...  18.8 us
    ppermute x8, starting transfers between devices, extended(): lax.ppermute(tail, axis, [(i, (i + 1) % count) for i in range(ends)])  17.3 us
    dot_general x2, matrix products, narrow_input_conv(): jnp.einsum('xyzk,kd->xyzd', columns, weight_mat, preferred_element_type=j...  16.4 us
    ppermute x8, waiting for transfers between devices, extended(): lax.ppermute(head, axis, [((i + 1) % count, i) for i in range(ends)])  15.8 us
  transfers between devices with their start and end apart: 20, of which 13 were waited for; matrix products, arithmetic and copies ran while one was open for 6% of the time, Pallas kernels for 0%

profile of v1, /device:TPU:0, one launch (start us, length us, event | category | flops | bytes accessed | tf_op | source)
XLA Modules:
  0.0 356.7 jit_solution(193349132666889652)
XLA Ops:
  7.5 4.9 %collective-permute-start = (bf16[32,1,16,16]{0,3,2,1:T(8,128)(2,1)S(1)}, bf16[32,1,16,16]{0,3,2,1:T(8,128)(2,1)S(1)}, u32[]{:S(2)}, u32[]{:S(2)}) collective-permute-start(bf16[32,1,16,16]{0,3,2,1:T(8,128)(2,1)S(1)} %get-tuple-element.14), channel_id=1, source_target_pairs={{0,2},{2,4},{4,6},{6,8},{8,10},{10,12},{12,14},{1,3},{3,5},{5,7},{... | collective-permute-start | bytes 49160 | tf_op jit(solution)/shard_map/ppermute | solution.py:17
  12.4 1.3 collective-permute-start.1
  15.4 3.2 collective-permute-done.1
  18.7 1.3 collective-permute-start.2
  20.0 1.3 collective-permute-start.3
  21.3 1.9 collective-permute-done.3
  25.0 2.8 reshape.84
  28.8 2.4 fusion.20
  32.7 12.9 %all_to_all.64 = bf16[4,8,2048]{2,0,1:T(4,128)(2,1)S(1)} all-to-all(bf16[4,8,2048]{2,0,1:T(4,128)(2,1)S(1)} %copy.47), channel_id=1, replica_groups=mesh['groups'=2,'wide'=8,'narrow'=2] {'wide'}, dimensions={1} | all-to-all | bytes 262144 | tf_op jit(solution)/shard_map/all_to_all | solution.py:66
  45.6 3.7 %fusion.129 = f32[32,1024]{1,0:T(8,128)} fusion(bf16[32,2048]{1,0:T(8,128)(2,1)S(1)} %all_to_all.51, bf16[2048,1024]{1,0:T(8,128)(2,1)} %param.12), kind=kOutput, calls=%fused_computation.270 | convolution fusion | flops 134217728 | bytes 4456448 | tf_op jit(solution)/shard_map/dot_general | solution.py:143
  50.0 37.7 %all-gather.9.cloned.1.call-done = f32[256,1024]{1,0:T(8,128)} async-done(((f32[32,1024]{1,0:T(8,128)}), f32[256,1024]{1,0:T(8,128)}) %all-gather.9.cloned.1.call-update) | async-done | bytes 1048592 | tf_op jit(solution)/shard_map/all_gather | solution.py:138
  87.7 1.3 reduce_sum.36
  89.1 1.3 collective-permute-start.4
  90.4 1.3 collective-permute-start.5
  91.7 18.6 %copy.51 = bf16[27,1024,256]{1,2,0:T(8,128)(2,1)} copy(bf16[27,1024,256]{2,1,0:T(8,128)(2,1)} %param.13) | data formatting | bytes 28311552 | tf_op args[4]
  110.3 9.4 %fusion.50 = f32[8,2,4,6912]{3,0,2,1:T(8,128)S(1)} fusion(bf16[1024,6912,1,1]{0,1,3,2:T(8,128)(2,1)} %bitcast.122, bf16[8,2,1,1024]{3,0,2,1:T(8,128)(2,1)S(1)} %collective-permute-done.5, bf16[8,2,2,1024]{3,0,2,1:T(8,128)(2,1)S(1)} %copy.48, bf16[8,2,1,1024]{3,0,2,1:T(8,128)(2,1)S(1)} %collective-permute-done.4), kind=kOutput, calls=%fused_computation.119 | convolution fusion | flops 906100736 | bytes 16056320 | tf_op jit(solution)/shard_map/xyzd,dk->xyzk/dot_general | solution.py:83
  119.8 3.0 collective-permute-start.6
  122.9 1.5 collective-permute-start.7
  124.3 1.6 collective-permute-done.7
  126.9 8.2 %fusion.130 = f32[32,1024]{1,0:T(8,128)} fusion(bf16[32,6912]{1,0:T(8,128)(2,1)S(1)} %reshape.75, bf16[6912,1024]{1,0:T(8,128)(2,1)} %bitcast.124), kind=kOutput, calls=%fused_computation.271 | convolution fusion | flops 452984832 | bytes 14729216 | tf_op jit(solution)/shard_map/xyzk,kd->xyzd/dot_general | solution.py:111
  135.2 39.0 %all-gather.11.cloned.1.call-done = f32[256,1024]{1,0:T(8,128)} async-done(((f32[32,1024]{1,0:T(8,128)}), f32[256,1024]{1,0:T(8,128)}) %all-gather.11.cloned.1.call-update) | async-done | bytes 1048592 | tf_op jit(solution)/shard_map/all_gather | solution.py:138
  175.5 3.0 convolution_convert_fusion.1
  178.6 10.6 %all_to_all.65 = bf16[8,4,2048]{2,1,0:T(4,128)(2,1)S(1)} all-to-all(bf16[8,4,2048]{2,1,0:T(4,128)(2,1)S(1)} %all_to_all.52), channel_id=1, replica_groups=mesh['groups'=2,'wide'=8,'narrow'=2] {'wide'}, dimensions={0} | all-to-all | bytes 262144 | tf_op jit(solution)/shard_map/all_to_all | solution.py:70
  189.2 1.3 reshape.108
  190.6 1.4 copy.54
  193.5 9.7 %all_to_all.66 = bf16[4,8,2048]{2,0,1:T(4,128)(2,1)S(1)} all-to-all(bf16[4,8,2048]{2,0,1:T(4,128)(2,1)S(1)} %copy.56), channel_id=1, replica_groups=mesh['groups'=2,'wide'=8,'narrow'=2] {'wide'}, dimensions={1} | all-to-all | bytes 262144 | tf_op jit(solution)/shard_map/all_to_all | solution.py:66
  203.2 4.2 %fusion.131 = f32[32,1024]{1,0:T(8,128)} fusion(bf16[32,2048]{1,0:T(8,128)(2,1)S(1)} %all_to_all.57, bf16[1024,2048]{1,0:T(8,128)(2,1)} %param.16), kind=kOutput, calls=%fused_computation.272 | convolution fusion | flops 134217728 | bytes 4456448 | tf_op jit(solution)/shard_map/nk,dk->nd/dot_general | solution.py:157
  207.5 38.0 %all-gather.13.cloned.1.call-done = f32[256,1024]{1,0:T(8,128)} async-done(((f32[32,1024]{1,0:T(8,128)}), f32[256,1024]{1,0:T(8,128)}) %all-gather.13.cloned.1.call-update) | async-done | bytes 1048592 | tf_op jit(solution)/shard_map/all_gather | solution.py:138
  246.9 1.3 collective-permute-start.8
  248.2 1.3 collective-permute-start.9
  249.5 1.8 collective-permute-done.9
  251.3 9.4 %fusion.56 = f32[8,2,4,6912]{3,0,2,1:T(8,128)S(1)} fusion(bf16[1024,6912,1,1]{0,1,3,2:T(8,128)(2,1)} %bitcast.125, bf16[8,2,1,1024]{3,0,2,1:T(8,128)(2,1)S(1)} %collective-permute-done.9, bf16[8,2,2,1024]{3,0,2,1:T(8,128)(2,1)S(1)} %copy.57, bf16[8,2,1,1024]{3,0,2,1:T(8,128)(2,1)S(1)} %collective-permute-done.8), kind=kOutput, calls=%fused_computation.125 | convolution fusion | flops 906100736 | bytes 16056320 | tf_op jit(solution)/shard_map/xyzd,dk->xyzk/dot_general | solution.py:83
  260.8 2.1 collective-permute-start.10
  262.9 1.5 collective-permute-start.11
  264.4 1.5 collective-permute-done.11
  266.9 8.2 %fusion.132 = f32[32,1024]{1,0:T(8,128)} fusion(bf16[32,6912]{1,0:T(8,128)(2,1)S(1)} %reshape.79, bf16[6912,1024]{1,0:T(8,128)(2,1)} %bitcast.123), kind=kOutput, calls=%fused_computation.273 | convolution fusion | flops 452984832 | bytes 14729216 | tf_op jit(solution)/shard_map/xyzk,kd->xyzd/dot_general | solution.py:111
  275.1 39.1 %all-gather.15.cloned.1.call-done = f32[256,1024]{1,0:T(8,128)} async-done(((f32[32,1024]{1,0:T(8,128)}), f32[256,1024]{1,0:T(8,128)}) %all-gather.15.cloned.1.call-update) | async-done | bytes 1048592 | tf_op jit(solution)/shard_map/all_gather | solution.py:138
  315.5 3.5 convolution_convert_fusion
  319.1 10.5 %all_to_all.67 = bf16[8,4,2048]{2,1,0:T(4,128)(2,1)S(1)} all-to-all(bf16[8,4,2048]{2,1,0:T(4,128)(2,1)S(1)} %all_to_all.58), channel_id=1, replica_groups=mesh['groups'=2,'wide'=8,'narrow'=2] {'wide'}, dimensions={0} | all-to-all | bytes 262144 | tf_op jit(solution)/shard_map/all_to_all | solution.py:70
  329.6 1.4 reshape.109
  331.0 1.4 copy.63
  332.8 2.1 collective-permute-start.12
  335.0 1.3 collective-permute-start.13
  337.0 4.1 %collective-permute-done.13 = bf16[32,1,16,16]{0,2,3,1:T(8,128)(2,1)S(1)} collective-permute-done((bf16[32,1,16,16]{0,2,3,1:T(8,128)(2,1)S(1)}, bf16[32,1,16,16]{0,2,3,1:T(8,128)(2,1)S(1)}, u32[]{:S(2)}, u32[]{:S(2)}) %collective-permute-start.13) | collective-permute-done | bytes 16416 | tf_op jit(solution)/shard_map/ppermute | solution.py:19
  341.1 1.3 collective-permute-start.14
  342.4 1.3 collective-permute-start.15
  343.8 1.8 collective-permute-done.15
  346.8 2.3 select_convert_fusion
  (137 shorter events, 18.1 us)
Async XLA Ops:
  6.5 85.1 %copy-start = (f32[1000,256]{1,0:T(8,128)S(1)}, f32[1000,256]{1,0:T(8,128)}, u32[]{:S(2)}) copy-start(f32[1000,256]{1,0:T(8,128)} %param.14) | copy-start | bytes 3072004
  6.5 81.1 %all-gather.9.cloned.1.call-start = ((), (), s32[]{:S(2)}) async-start(), calls=%async_computation.4 | async-start | bytes 1179648 | tf_op jit(solution)/shard_map/all_gather | solution.py:138
  7.5 6.8 %collective-permute-start = (bf16[32,1,16,16]{0,3,2,1:T(8,128)(2,1)S(1)}, bf16[32,1,16,16]{0,3,2,1:T(8,128)(2,1)S(1)}, u32[]{:S(2)}, u32[]{:S(2)}) collective-permute-start(bf16[32,1,16,16]{0,3,2,1:T(8,128)(2,1)S(1)} %get-tuple-element.14), channel_id=1, source_target_pairs={{0,2},{2,4},{4,6},{6,8},{8,10},{10,12},{12,14},{1,3},{3,5},{5,7},{... | collective-permute-start | bytes 49160 | tf_op jit(solution)/shard_map/ppermute | solution.py:17
  12.4 6.2 %collective-permute-start.1 = (bf16[32,1,16,16]{0,3,2,1:T(8,128)(2,1)S(1)}, bf16[32,1,16,16]{0,3,2,1:T(8,128)(2,1)S(1)}, u32[]{:S(2)}, u32[]{:S(2)}) collective-permute-start(bf16[32,1,16,16]{0,3,2,1:T(8,128)(2,1)S(1)} %get-tuple-element.13), channel_id=1, source_target_pairs={{2,0},{4,2},{6,4},{8,6},{10,8},{12,10},{14,12},{3,1},{5,3},{7,5},{... | collective-permute-start | bytes 49160 | tf_op jit(solution)/shard_map/ppermute | solution.py:19
  18.7 2.6 collective-permute-start.2
  20.0 3.2 collective-permute-start.3
  27.9 0.9 copy-start.3
  27.9 0.9 copy-start.4
  49.3 124.9 %all-gather.11.cloned.1.call-start = ((), (), s32[]{:S(2)}) async-start(), calls=%async_computation.5 | async-start | bytes 1179648 | tf_op jit(solution)/shard_map/all_gather | solution.py:138
  89.1 21.3 %collective-permute-start.4 = (bf16[8,2,1,1024]{3,0,2,1:T(8,128)(2,1)S(1)}, bf16[8,2,1,1024]{3,0,2,1:T(8,128)(2,1)S(1)}, u32[]{:S(2)}, u32[]{:S(2)}) collective-permute-start(bf16[8,2,1,1024]{3,0,2,1:T(8,128)(2,1)S(1)} %get-tuple-element.17), channel_id=1, source_target_pairs={{0,1},{2,3},{4,5},{6,7},{8,9},{10,11},{12,13},{14,15},{16,17},{18,... | collective-permute-start | bytes 98312 | tf_op jit(solution)/shard_map/ppermute | solution.py:17
  90.4 20.0 %collective-permute-start.5 = (bf16[8,2,1,1024]{3,0,2,1:T(8,128)(2,1)S(1)}, bf16[8,2,1,1024]{3,0,2,1:T(8,128)(2,1)S(1)}, u32[]{:S(2)}, u32[]{:S(2)}) collective-permute-start(bf16[8,2,1,1024]{3,0,2,1:T(8,128)(2,1)S(1)} %get-tuple-element.18), channel_id=1, source_target_pairs={{1,0},{3,2},{5,4},{7,6},{9,8},{11,10},{13,12},{15,14},{17,16},{19,... | collective-permute-start | bytes 98312 | tf_op jit(solution)/shard_map/ppermute | solution.py:19
  119.8 4.5 %collective-permute-start.6 = (bf16[8,2,1,256]{3,0,2,1:T(8,128)(2,1)S(1)}, bf16[8,2,1,256]{3,0,2,1:T(8,128)(2,1)S(1)}, u32[]{:S(2)}, u32[]{:S(2)}) collective-permute-start(bf16[8,2,1,256]{3,0,2,1:T(8,128)(2,1)S(1)} %get-tuple-element.21), channel_id=1, source_target_pairs={{0,1},{2,3},{4,5},{6,7},{8,9},{10,11},{12,13},{14,15},{16,17},{18,... | collective-permute-start | bytes 24584 | tf_op jit(solution)/shard_map/ppermute | solution.py:17
  122.9 3.1 collective-permute-start.7
  135.1 110.4 %all-gather.13.cloned.1.call-start = ((), (), s32[]{:S(2)}) async-start(), calls=%async_computation.6 | async-start | bytes 1179648 | tf_op jit(solution)/shard_map/all_gather | solution.py:138
  178.5 13.5 %copy-start.2 = (bf16[32,8,16,16]{0,3,2,1:T(8,128)(2,1)S(1)}, bf16[32,8,16,16]{0,3,2,1:T(8,128)(2,1)}, u32[]{:S(2)}) copy-start(bf16[32,8,16,16]{0,3,2,1:T(8,128)(2,1)} %param.10) | copy-start | bytes 393220
  207.5 106.7 %all-gather.15.cloned.1.call-start = ((), (), s32[]{:S(2)}) async-start(), calls=%async_computation.7 | async-start | bytes 1179648 | tf_op jit(solution)/shard_map/all_gather | solution.py:138
  246.9 2.6 collective-permute-start.8
  248.2 3.1 collective-permute-start.9
  260.8 3.6 %collective-permute-start.10 = (bf16[8,2,1,256]{3,0,2,1:T(8,128)(2,1)S(1)}, bf16[8,2,1,256]{3,0,2,1:T(8,128)(2,1)S(1)}, u32[]{:S(2)}, u32[]{:S(2)}) collective-permute-start(bf16[8,2,1,256]{3,0,2,1:T(8,128)(2,1)S(1)} %get-tuple-element.19), channel_id=1, source_target_pairs={{0,1},{2,3},{4,5},{6,7},{8,9},{10,11},{12,13},{14,15},{16,17},{18,... | collective-permute-start | bytes 24584 | tf_op jit(solution)/shard_map/ppermute | solution.py:17
  262.9 3.1 collective-permute-start.11
  332.8 4.2 %collective-permute-start.12 = (bf16[32,1,16,16]{0,2,3,1:T(8,128)(2,1)S(1)}, bf16[32,1,16,16]{0,2,3,1:T(8,128)(2,1)S(1)}, u32[]{:S(2)}, u32[]{:S(2)}) collective-permute-start(bf16[32,1,16,16]{0,2,3,1:T(8,128)(2,1)S(1)} %get-tuple-element.11), channel_id=1, source_target_pairs={{0,2},{2,4},{4,6},{6,8},{8,10},{10,12},{12,14},{1,3},{3,5},{5,7},{... | collective-permute-start | bytes 49160 | tf_op jit(solution)/shard_map/ppermute | solution.py:17
  335.0 6.2 %collective-permute-start.13 = (bf16[32,1,16,16]{0,2,3,1:T(8,128)(2,1)S(1)}, bf16[32,1,16,16]{0,2,3,1:T(8,128)(2,1)S(1)}, u32[]{:S(2)}, u32[]{:S(2)}) collective-permute-start(bf16[32,1,16,16]{0,2,3,1:T(8,128)(2,1)S(1)} %get-tuple-element.12), channel_id=1, source_target_pairs={{2,0},{4,2},{6,4},{8,6},{10,8},{12,10},{14,12},{3,1},{5,3},{7,5},{... | collective-permute-start | bytes 49160 | tf_op jit(solution)/shard_map/ppermute | solution.py:19
  341.1 2.6 collective-permute-start.14
  342.4 3.1 collective-permute-start.15
  346.8 3.4 copy-start.1
Sparse Core Ops, SparseCore 0:
  49.4 38.2 all-gather.8
  135.3 38.8 all-gather.10
  207.6 37.8 all-gather.12
  275.3 38.8 all-gather.14
